TPU v7x, 128 devices: a whole 4x4x4 slice. The times are simulated.
128 devices in a mesh: node: 16 (over x, z), local: 8 (over y, core).
Axes of the slice: x: 4, y: 4, z: 4, core: 2. Of those that a mesh axis runs over, the one named last changes fastest.
Arguments:
- tokens: bfloat16 [32768, 7168], P(('node', 'local')), may hold values from -6 to 6
- out_grad: bfloat16 [32768, 7168], P(('node', 'local')), may hold values from -6 to 6
- route_ids: int32 [32768, 8], P(('node', 'local')), may hold values from 0 to 383, as said below
- route_gates: bfloat16 [32768, 8], P(('node', 'local')), may hold values from 0.049804688 to 0.5
- w_gate: bfloat16 [16, 7168, 1024], P('node', None, 'local'), may hold values from -0.0625 to 0.0625
- w_up: bfloat16 [16, 7168, 1024], P('node', None, 'local'), may hold values from -0.0625 to 0.0625
- w_down: bfloat16 [16, 1024, 7168], P('node', 'local'), may hold values from -0.1875 to 0.1875
Outputs:
- token_grad: bfloat16 [32768, 7168], P(('node', 'local'))
- gate_grad: float32 [32768, 8], P(('node', 'local'))
- grad_w_gate: bfloat16 [16, 7168, 1024], P('node', None, 'local')
- grad_w_up: bfloat16 [16, 7168, 1024], P('node', None, 'local')
- grad_w_down: bfloat16 [16, 1024, 7168], P('node', 'local')
Inputs may be any that keep to these rules, and one draw needn't show every extreme that they name: `route_ids`: each row names 8 different experts, at most one of them below 16. Among the 256 rows of one device at most 4 name any one expert below 16; in every draw one expert below 16 is named by exactly 4 rows of every device.
All inputs are finite; a program needn't handle non-finite values.
Results may differ from a plain program's by a relative error of at most 0.0058.
Values may be sent and summed in bfloat16 or wider, within the bound.
A program may use at most 192 MiB of HBM per device.

v0:
```python
import jax
import jax.numpy as jnp
from jax import lax
from jax.sharding import PartitionSpec as P

CAP = 4


def contract_rows(left, right):
    return lax.dot_general(
        left, right, (((0,), (0,)), ((), ())), preferred_element_type=jnp.float32
    )


def contract_cols(left, right):
    return lax.dot_general(
        left, right, (((1,), (1,)), ((), ())), preferred_element_type=jnp.float32
    )


def spread_copies(array, copies):
    widened = jnp.broadcast_to(array[:, None], (array.shape[0], copies) + array.shape[1:])
    return widened.reshape((array.shape[0] * copies,) + array.shape[1:])


def body(tokens, out_grad, route_ids, route_gates, w_gate, w_up, w_down):
    node_count = lax.axis_size("node")
    local_count = lax.axis_size("local")
    width = tokens.shape[1]
    is_held = route_ids < node_count
    expert = jnp.sum(jnp.where(is_held, route_ids, 0), axis=1)
    inside = jnp.any(is_held, axis=1)
    tok_gate = jnp.sum(jnp.where(is_held, route_gates.astype(jnp.float32), 0.0), axis=1)
    one_hot = ((expert[:, None] == jnp.arange(node_count)[None, :]) & inside[:, None]).astype(
        jnp.int32
    )
    earlier = jnp.cumsum(one_hot, axis=0) - one_hot
    slot_index = jnp.sum(earlier * one_hot, axis=1)
    target = jnp.where(inside, expert * CAP + slot_index, -1)
    picker = (jnp.arange(node_count * CAP)[:, None] == target[None, :]).astype(jnp.bfloat16)
    sent_rows = (
        jnp.dot(picker, tokens, preferred_element_type=jnp.float32)
        .astype(jnp.bfloat16)
        .reshape(node_count, CAP, width)
    )
    sent_grads = (
        jnp.dot(picker, out_grad, preferred_element_type=jnp.float32)
        .astype(jnp.bfloat16)
        .reshape(node_count, CAP, width)
    )
    sent_gates = (
        jnp.dot(picker, tok_gate.astype(jnp.bfloat16)[:, None], preferred_element_type=jnp.float32)[
            :, 0
        ]
        .astype(jnp.bfloat16)
        .reshape(node_count, CAP)
    )
    got_rows, got_grads, got_gates = (
        lax.all_to_all(
            spread_copies(sent_rows, local_count),
            ("node", "local"),
            split_axis=0,
            concat_axis=0,
            tiled=True,
        ),
        lax.all_to_all(
            spread_copies(sent_grads, local_count),
            ("node", "local"),
            split_axis=0,
            concat_axis=0,
            tiled=True,
        ),
        lax.all_to_all(
            spread_copies(sent_gates, local_count),
            ("node", "local"),
            split_axis=0,
            concat_axis=0,
            tiled=True,
        ),
    )
    row_count = node_count * local_count * CAP
    in_rows = got_rows.reshape(row_count, width)
    in_grads = got_grads.reshape(row_count, width)
    in_gates = got_gates.reshape(row_count)
    gate_mat = w_gate[0]
    up_mat = w_up[0]
    down_mat = w_down[0]
    gate_pre = jnp.dot(in_rows, gate_mat, preferred_element_type=jnp.float32)
    up_pre = jnp.dot(in_rows, up_mat, preferred_element_type=jnp.float32)
    logistic = jax.nn.sigmoid(gate_pre)
    hidden = (gate_pre * logistic * up_pre).astype(jnp.bfloat16)
    expert_out = jnp.dot(hidden, down_mat, preferred_element_type=jnp.float32)
    part_scores = jnp.sum(expert_out * in_grads, axis=1)
    scaled_grad = (in_gates.astype(jnp.float32)[:, None] * in_grads).astype(jnp.bfloat16)
    hidden_grad = contract_cols(scaled_grad, down_mat)
    gate_delta = (hidden_grad * up_pre * logistic * (1.0 + gate_pre * (1.0 - logistic))).astype(
        jnp.bfloat16
    )
    up_delta = (hidden_grad * gate_pre * logistic).astype(jnp.bfloat16)
    grad_down = contract_rows(hidden, scaled_grad).astype(jnp.bfloat16)
    grad_gate = contract_rows(in_rows, gate_delta).astype(jnp.bfloat16)
    grad_up = contract_rows(in_rows, up_delta).astype(jnp.bfloat16)
    row_grads = contract_cols(gate_delta, gate_mat) + contract_cols(up_delta, up_mat)
    share_rows = row_grads.reshape(node_count, local_count, CAP, width)
    share_scores = part_scores.reshape(node_count, local_count, CAP)
    back_rows, back_scores = (
        lax.all_to_all(
            share_rows.reshape(node_count * local_count, CAP, width),
            ("node", "local"),
            split_axis=0,
            concat_axis=0,
            tiled=True,
        ),
        lax.all_to_all(
            share_scores.reshape(node_count * local_count, CAP),
            ("node", "local"),
            split_axis=0,
            concat_axis=0,
            tiled=True,
        ),
    )
    summed_rows = jnp.sum(back_rows.reshape(node_count, local_count, CAP, width), axis=1)
    summed_scores = jnp.sum(back_scores.reshape(node_count, local_count, CAP), axis=1)
    slot_rows = summed_rows.reshape(node_count * CAP, width)
    slot_scores = summed_scores.reshape(node_count * CAP)
    safe_slot = jnp.maximum(target, 0)
    token_sum = jnp.where(inside[:, None], slot_rows[safe_slot], 0.0)
    token_grad = token_sum.astype(jnp.bfloat16)
    tok_score = jnp.where(inside, slot_scores[safe_slot], 0.0)
    gate_grad = jnp.where(is_held, tok_score[:, None], 0.0)
    return (token_grad, gate_grad, grad_gate[None], grad_up[None], grad_down[None])


def solution(mesh):
    return jax.shard_map(
        body,
        mesh=mesh,
        in_specs=(
            P(("node", "local"), None),
            P(("node", "local"), None),
            P(("node", "local"), None),
            P(("node", "local"), None),
            P("node", None, "local"),
            P("node", None, "local"),
            P("node", "local", None),
        ),
        out_specs=(
            P(("node", "local"), None),
            P(("node", "local"), None),
            P("node", None, "local"),
            P("node", None, "local"),
            P("node", "local", None),
        ),
        check_vma=False,
    )
```

profile of v0, /device:TPU:114, one launch (start us, length us, event | category | flops | bytes accessed | tf_op | source)
XLA Modules:
  0.0 553.0 jit_solution(12349369537192649288)
XLA Ops:
  4.5 9.7 %all-to-all-start = ((bf16[128,1,4]{2,1,0:T(2,128)(2,1)}), bf16[128,1,4]{2,1,0:T(2,128)(2,1)S(1)}, u32[]{:S(2)}, u32[]{:S(2)}) async-start(bf16[128,1,4]{2,1,0:T(2,128)(2,1)} %copy.17), calls=%async_computation | async-start | bytes 131072 | tf_op jit(solution)/shard_map/all_to_all | solution.py:73
  18.8 6.3 %broadcast_in_dim.83 = bf16[16,8,4,7168]{3,2,1,0:T(4,128)(2,1)} broadcast(bf16[16,4,7168]{2,1,0:T(4,128)(2,1)} %broadcast_in_dim.82), dimensions={0,2,3} | broadcast | bytes 8257536 | tf_op jit(solution)/shard_map/broadcast_in_dim | solution.py:22
  25.2 10.4 %all-to-all-start.1 = ((bf16[128,4,7168]{2,1,0:T(4,128)(2,1)}), bf16[128,4,7168]{2,1,0:T(4,128)(2,1)}, u32[]{:S(2)}, u32[]{:S(2)}) async-start(bf16[128,4,7168]{2,1,0:T(4,128)(2,1)} %bitcast.76), calls=%async_computation.1 | async-start | bytes 14680064 | tf_op jit(solution)/shard_map/all_to_all | solution.py:66
  39.6 82.8 %all-to-all-done.1 = bf16[128,4,7168]{2,1,0:T(4,128)(2,1)} async-done(((bf16[128,4,7168]{2,1,0:T(4,128)(2,1)}), bf16[128,4,7168]{2,1,0:T(4,128)(2,1)}, u32[]{:S(2)}, u32[]{:S(2)}) %all-to-all-start.1) | async-done | bytes 7340064 | tf_op jit(solution)/shard_map/all_to_all | solution.py:66
  122.4 6.4 %broadcast_in_dim.85 = bf16[16,8,4,7168]{3,2,1,0:T(4,128)(2,1)} broadcast(bf16[16,4,7168]{2,1,0:T(4,128)(2,1)} %broadcast_in_dim.84), dimensions={0,2,3} | broadcast | bytes 8257536 | tf_op jit(solution)/shard_map/broadcast_in_dim | solution.py:22
  128.8 14.5 %all-to-all-start.2 = ((bf16[128,4,7168]{2,1,0:T(4,128)(2,1)}), bf16[128,4,7168]{2,1,0:T(4,128)(2,1)}, u32[]{:S(2)}, u32[]{:S(2)}) async-start(bf16[128,4,7168]{2,1,0:T(4,128)(2,1)} %bitcast.75), calls=%async_computation.2 | async-start | bytes 14680064 | tf_op jit(solution)/shard_map/all_to_all | solution.py:59
  143.4 9.6 %multiply_convert_fusion.1 = bf16[128,4,7168]{2,1,0:T(4,128)(2,1)} fusion(f32[128,4]{1,0:T(8,128)S(1)} %bitcast.77, bf16[128,4,7168]{2,1,0:T(4,128)(2,1)} %all-to-all-done.1), kind=kLoop, calls=%fused_computation.5 | loop fusion | flops 11010048 | bytes 14682112 | tf_op jit(solution)/shard_map/convert_element_type | solution.py:94
  152.9 12.1 %convert_element_type.98 = bf16[512,7168]{1,0:T(8,128)(2,1)} reshape(bf16[128,4,7168]{2,1,0:T(4,128)(2,1)} %multiply_convert_fusion.1) | data formatting | bytes 14680064 | tf_op jit(solution)/shard_map/convert_element_type | solution.py:94
  165.0 64.7 %all-to-all-done.2 = bf16[128,4,7168]{2,1,0:T(4,128)(2,1)} async-done(((bf16[128,4,7168]{2,1,0:T(4,128)(2,1)}), bf16[128,4,7168]{2,1,0:T(4,128)(2,1)}, u32[]{:S(2)}, u32[]{:S(2)}) %all-to-all-start.2) | async-done | bytes 7340064 | tf_op jit(solution)/shard_map/all_to_all | solution.py:59
  229.7 12.1 %reshape.141 = bf16[512,7168]{1,0:T(8,128)(2,1)} reshape(bf16[128,4,7168]{2,1,0:T(4,128)(2,1)} %all-to-all-done.2) | data formatting | bytes 14680064 | tf_op jit(solution)/shard_map/reshape | solution.py:82
  241.8 5.8 %fusion.6 = f32[512,128]{1,0:T(8,128)S(1)} fusion(bf16[512,7168]{1,0:T(8,128)(2,1)} %reshape.141, bf16[1,7168,128]{2,1,0:T(8,128)(2,1)} %param.11), kind=kOutput, calls=%fused_computation.19 | convolution fusion | flops 939524096 | bytes 9437184 | tf_op jit(solution)/shard_map/dot_general | solution.py:88
  247.6 5.3 fusion.12
  255.1 13.2 %reshape.147 = f32[512,7168]{1,0:T(8,128)} reshape(bf16[128,4,7168]{2,1,0:T(4,128)(2,1)} %all-to-all-done.1) | data formatting | bytes 22020096 | tf_op jit(solution)/shard_map/convert_element_type | solution.py:94
  268.3 7.9 %multiply_reduce_fusion = f32[512]{0:T(512)S(1)} fusion(f32[512,7168]{1,0:T(8,128)} %reshape.147, bf16[512,128]{1,0:T(8,128)(2,1)S(1)} %get-tuple-element.9, bf16[1,128,7168]{2,1,0:T(8,128)(2,1)} %param.13), kind=kOutput, calls=%fused_computation.4 | convolution fusion | flops 946863616 | bytes 16648192 | tf_op jit(solution)/shard_map/dot_general | solution.py:92
  276.9 12.2 %all-to-all-start.4 = ((f32[128,1,4]{2,1,0:T(1,128)}), f32[128,1,4]{2,1,0:T(1,128)S(1)}, u32[]{:S(2)}, u32[]{:S(2)}) async-start(f32[128,1,4]{2,1,0:T(1,128)} %bitcast.11), calls=%async_computation.4 | async-start | bytes 131072 | tf_op jit(solution)/shard_map/all_to_all | solution.py:114
  292.7 7.3 %convolution_add_fusion = f32[512,7168]{1,0:T(8,128)} fusion(f32[512,7168]{1,0:T(8,128)S(1)} %fusion.4, bf16[512,128]{1,0:T(8,128)(2,1)S(1)} %get-tuple-element.11, bf16[1,7168,128]{2,1,0:T(8,128)(2,1)S(1)} %copy-done), kind=kOutput, calls=%fused_computation.6 | convolution fusion | flops 943194112 | bytes 31326208 | tf_op jit(solution)/shard_map/dot_general | solution.py:16
  300.0 17.0 %reshape_reshape.4 = f32[128,4,7168]{2,1,0:T(4,128)} reshape(f32[512,7168]{1,0:T(8,128)} %convolution_add_fusion) | data formatting | bytes 29360128 | tf_op jit(solution)/shard_map/reshape;reshape | solution.py:108
  317.0 10.6 %all-to-all-start.3 = ((f32[128,4,7168]{2,1,0:T(4,128)}), f32[128,4,7168]{2,1,0:T(4,128)}, u32[]{:S(2)}, u32[]{:S(2)}) async-start(f32[128,4,7168]{2,1,0:T(4,128)} %reshape_reshape.4), calls=%async_computation.3 | async-start | bytes 29360128 | tf_op jit(solution)/shard_map/all_to_all | solution.py:107
  327.9 6.5 %fusion = bf16[1,7168,128]{2,1,0:T(8,128)(2,1)} fusion(bf16[512,7168]{1,0:T(8,128)(2,1)} %reshape.141, bf16[512,128]{1,0:T(8,128)(2,1)S(1)} %get-tuple-element.10), kind=kOutput, calls=%fused_computation.10 | convolution fusion | flops 940441600 | bytes 9306112 | tf_op jit(solution)/shard_map/dot_general | solution.py:10
  334.3 6.4 %fusion.1 = bf16[1,7168,128]{2,1,0:T(8,128)(2,1)} fusion(bf16[512,7168]{1,0:T(8,128)(2,1)} %reshape.141, bf16[512,128]{1,0:T(8,128)(2,1)S(1)} %get-tuple-element.11), kind=kOutput, calls=%fused_computation.11 | convolution fusion | flops 940441600 | bytes 9306112 | tf_op jit(solution)/shard_map/dot_general | solution.py:10
  340.8 8.2 %fusion.2 = bf16[1,128,7168]{2,1,0:T(8,128)(2,1)} fusion(bf16[512,128]{1,0:T(8,128)(2,1)S(1)} %get-tuple-element.9, f32[512,7168]{1,0:T(8,128)} %reshape.147, f32[512]{0:T(512)S(1)} %reshape.148), kind=kOutput, calls=%fused_computation.12 | convolution fusion | flops 947781632 | bytes 16648192 | tf_op jit(solution)/shard_map/dot_general | solution.py:10
  351.6 182.5 %all-to-all-done.3 = f32[128,4,7168]{2,1,0:T(4,128)} async-done(((f32[128,4,7168]{2,1,0:T(4,128)}), f32[128,4,7168]{2,1,0:T(4,128)}, u32[]{:S(2)}, u32[]{:S(2)}) %all-to-all-start.3) | async-done | bytes 14680096 | tf_op jit(solution)/shard_map/all_to_all | solution.py:107
  534.1 9.0 %bitcast_reduce_fusion = bf16[16,4,7168]{2,1,0:T(4,128)(2,1)S(1)} fusion(f32[128,4,7168]{2,1,0:T(4,128)} %all-to-all-done.3), kind=kLoop, calls=%fused_computation.2 | loop fusion | flops 3211264 | bytes 15597568 | tf_op jit(solution)/shard_map/reduce_sum | solution.py:122
  548.0 4.8 select_convert_fusion
  (48 shorter events, 26.8 us)
Async XLA Ops:
  0.6 252.3 %copy-start = (bf16[1,7168,128]{2,1,0:T(8,128)(2,1)S(1)}, bf16[1,7168,128]{2,1,0:T(8,128)(2,1)}, u32[]{:S(2)}) copy-start(bf16[1,7168,128]{2,1,0:T(8,128)(2,1)} %param.12) | copy-start | bytes 5505028
  4.5 14.4 %all-to-all-start = ((bf16[128,1,4]{2,1,0:T(2,128)(2,1)}), bf16[128,1,4]{2,1,0:T(2,128)(2,1)S(1)}, u32[]{:S(2)}, u32[]{:S(2)}) async-start(bf16[128,1,4]{2,1,0:T(2,128)(2,1)} %copy.17), calls=%async_computation | async-start | bytes 131072 | tf_op jit(solution)/shard_map/all_to_all | solution.py:73
  25.2 97.3 %all-to-all-start.1 = ((bf16[128,4,7168]{2,1,0:T(4,128)(2,1)}), bf16[128,4,7168]{2,1,0:T(4,128)(2,1)}, u32[]{:S(2)}, u32[]{:S(2)}) async-start(bf16[128,4,7168]{2,1,0:T(4,128)(2,1)} %bitcast.76), calls=%async_computation.1 | async-start | bytes 14680064 | tf_op jit(solution)/shard_map/all_to_all | solution.py:66
  128.8 100.9 %all-to-all-start.2 = ((bf16[128,4,7168]{2,1,0:T(4,128)(2,1)}), bf16[128,4,7168]{2,1,0:T(4,128)(2,1)}, u32[]{:S(2)}, u32[]{:S(2)}) async-start(bf16[128,4,7168]{2,1,0:T(4,128)(2,1)} %bitcast.75), calls=%async_computation.2 | async-start | bytes 14680064 | tf_op jit(solution)/shard_map/all_to_all | solution.py:59
  241.8 5.8 %copy-start.2 = (bf16[1,128,7168]{2,1,0:T(8,128)(2,1)S(1)}, bf16[1,128,7168]{2,1,0:T(8,128)(2,1)}, u32[]{:S(2)}) copy-start(bf16[1,128,7168]{2,1,0:T(8,128)(2,1)} %param.13) | copy-start | bytes 5505028
  241.8 11.2 %slice-start = ((s8[7340032]{0:T(1024)(128)(4,1)}), s8[4194304]{0:T(1024)(128)(4,1)S(1)}, s32[]{:S(2)}) async-start(s8[7340032]{0:T(1024)(128)(4,1)} %bitcast.73), calls=%async_computation.5 | async-start | bytes 8388608
  247.6 5.4 slice-start.1
  276.9 40.1 %all-to-all-start.4 = ((f32[128,1,4]{2,1,0:T(1,128)}), f32[128,1,4]{2,1,0:T(1,128)S(1)}, u32[]{:S(2)}, u32[]{:S(2)}) async-start(f32[128,1,4]{2,1,0:T(1,128)} %bitcast.11), calls=%async_computation.4 | async-start | bytes 131072 | tf_op jit(solution)/shard_map/all_to_all | solution.py:114
  317.0 217.1 %all-to-all-start.3 = ((f32[128,4,7168]{2,1,0:T(4,128)}), f32[128,4,7168]{2,1,0:T(4,128)}, u32[]{:S(2)}, u32[]{:S(2)}) async-start(f32[128,4,7168]{2,1,0:T(4,128)} %reshape_reshape.4), calls=%async_computation.3 | async-start | bytes 29360128 | tf_op jit(solution)/shard_map/all_to_all | solution.py:107
  543.3 9.5 %copy-start.1 = (bf16[1,7168,128]{2,1,0:T(8,128)(2,1)S(1)}, bf16[1,7168,128]{2,1,0:T(8,128)(2,1)}, u32[]{:S(2)}) copy-start(bf16[1,7168,128]{2,1,0:T(8,128)(2,1)} %param.12) | copy-start | bytes 5505028
where the time goes:
time: 561 us; the launch traced here: 553 us
  waiting for transfers between devices  331 us (59%)
  local copies, waits for them, and re-layouts  78.7 us (14%)
  matrix products  58.8 us (10%)
  starting transfers between devices  57.4 us (10%)
  other arithmetic  26.5 us (5%)
    all_to_all x1, waiting for transfers between devices, body(): lax.all_to_all(share_rows.reshape(node_count * local_count, CAP, width),...  183 us
    all_to_all x1, waiting for transfers between devices, body(): lax.all_to_all(spread_copies(sent_grads, local_count), ('node', 'local'),...  82.8 us
    all_to_all x1, waiting for transfers between devices, body(): lax.all_to_all(spread_copies(sent_rows, local_count), ('node', 'local'),...  64.7 us
    dot_general x3, matrix products, contract_rows(): lax.dot_general(left, right, (((0,), (0,)), ((), ())), preferred_element_...  21.1 us
    another operation x1, local copies, waits for them, and re-layouts, body(): share_rows.reshape(node_count * local_count, CAP, width)  17 us
    dot_general x3, matrix products, contract_cols(): lax.dot_general(left, right, (((1,), (1,)), ((), ())), preferred_element_...  16.2 us
    broadcast_in_dim x5, local copies, waits for them, and re-layouts, spread_copies(): jnp.broadcast_to(array[:, None], (array.shape[0], copies) + array.shape[1:])  15.3 us
    all_to_all x1, starting transfers between devices, body(): lax.all_to_all(spread_copies(sent_rows, local_count), ('node', 'local'),...  14.5 us
  transfers between devices with their start and end apart: 5, of which 4 were waited for; matrix products, arithmetic and copies ran while one was open for 15% of the time, Pallas kernels for 0%

commit v1 on v0

v1 whole, which is shorter than its diff:
```python
import functools

import jax
import jax.numpy as jnp
from jax import lax
from jax.experimental import pallas as pl
from jax.experimental.pallas import tpu as pltpu
from jax.sharding import PartitionSpec as P

MESH = pl.DeviceIdType.MESH
F32 = jnp.float32
BF16 = jnp.bfloat16

CAP = 4
TOK = 256
D = 7168
HALF = D // 2
QUART = D // 4
FFD = 128
NODES = 16
SIDE = 4
SCW = 128
RW = D + SCW
PH = 4
ROWS = 128


def iota(shape, dim):
    return lax.broadcasted_iota(jnp.int32, shape, dim)


def slot_targets(ids, gates):
    held = ids < NODES
    expert = jnp.sum(jnp.where(held, ids, 0).astype(F32), axis=1, keepdims=True)
    inside = jnp.sum(jnp.where(held, 1.0, 0.0), axis=1, keepdims=True) > 0.5
    gate = jnp.sum(jnp.where(held, gates.astype(F32), 0.0), axis=1, keepdims=True)
    lane = iota((TOK, 128), 1).astype(F32)
    one_hot = jnp.where((lane == expert) & inside, 1.0, 0.0)
    before = jnp.where(iota((TOK, TOK), 0) > iota((TOK, TOK), 1), 1.0, 0.0)
    ranks = jnp.dot(before.astype(BF16), one_hot.astype(BF16), preferred_element_type=F32)
    rank = jnp.sum(ranks * one_hot, axis=1, keepdims=True)
    target = jnp.where(inside, expert * CAP + rank, -1.0)
    return target, gate


def wanted(block, gx, gz):
    k = block >> 4
    p = k >> 2
    dx = p ^ (p >> 1)
    dz = k & 3
    node = ((gx - dx) & 3) * SIDE + ((gz - dz) & 3)
    return (node * CAP + (block & 3)).astype(F32), (block >> 2) & 3


def hi_lo(score):
    hi = score.astype(BF16).astype(F32)
    lane = iota(score.shape, 1)
    return jnp.where(lane < 64, hi, score - hi).astype(BF16)


def from_hi_lo(pair):
    wide = pair.astype(F32)
    return wide + pltpu.roll(wide, 64, 1)


def contract_cols(left, right):
    return lax.dot_general(left, right, (((1,), (1,)), ((), ())), preferred_element_type=F32)


def exchange_kernel(
    ids, gates, tok_hbm, og_hbm, wg_hbm, wu_hbm, wd_hbm,
    ret_hbm, gg_hbm, gu_hbm, gd_hbm,
    tok, og, pick, sraw, rraw, xg, wgu, wgup, wd,
    dl, dlt, hidt, score, psend, precv,
    rgf, o3s, o3r, j1s, j1r, j2s, j2r, fstk, rets, retr,
    ggo, guo, gdo, perm,
    ssem, rsem, lsem,
):
    node = lax.axis_index("node")
    loc = lax.axis_index("local")
    gx, gz = node // SIDE, node % SIDE
    y, c = loc // 2, loc % 2
    up = (node, ((y + 1) % 4) * 2 + c)
    down = (node, ((y + 3) % 4) * 2 + c)
    other = (node, y * 2 + 1 - c)

    def gray(k):
        p = k // 4
        return p ^ (p >> 1), k % 4

    def dest(k):
        dx, dz = gray(k)
        return (((gx + 4 - dx) % 4) * SIDE + (gz + 4 - dz) % 4, loc)

    def source(k):
        dx, dz = gray(k)
        return (((gx + dx) % 4) * SIDE + (gz + dz) % 4, loc)

    local = []

    def load(src, dst):
        copy = pltpu.make_async_copy(src, dst, lsem.at[len(local)])
        local.append(copy)
        copy.start()
        return copy

    ld_tok = load(tok_hbm, tok)
    ld_og = load(og_hbm, og)
    ld_wg = load(wg_hbm, wgu.at[:, pl.ds(0, FFD)])
    ld_wu = load(wu_hbm, wgu.at[:, pl.ds(FFD, FFD)])
    ld_wd = load(wd_hbm, wd)

    barrier = pltpu.get_barrier_semaphore()
    partners = [up, down, other] + [dest(k) for k in range(1, NODES)]
    for who in partners:
        pl.semaphore_signal(barrier, inc=1, device_id=who, device_id_type=MESH)

    remote = []

    def send(src, dst, who):
        i = len(remote)
        copy = pltpu.make_async_remote_copy(
            src_ref=src, dst_ref=dst, send_sem=ssem.at[i], recv_sem=rsem.at[i],
            device_id=who, device_id_type=MESH,
        )
        remote.append(copy)
        copy.start()
        return copy

    target, gate = slot_targets(ids[...], gates[...])
    eye = iota((TOK, TOK), 0) == iota((TOK, TOK), 1)
    target_row = jnp.sum(jnp.where(eye, target, 0.0), axis=0, keepdims=True)
    gate_row = jnp.sum(jnp.where(eye, gate, 0.0), axis=0, keepdims=True)
    want, quarter = wanted(iota((TOK, TOK), 0), gx, gz)
    hit = want == target_row
    for q in range(4):
        chosen = hit & (quarter == q)
        pick[q] = jnp.where(chosen, 1.0, 0.0).astype(BF16)
        pick[4 + q] = jnp.where(chosen, gate_row, 0.0).astype(BF16)
    pi, pj = iota((64, 64), 0), iota((64, 64), 1)
    swapped = ((pj >> 2) & 3) * 16 + (pj >> 4) * 4 + (pj & 3)
    perm[...] = jnp.where(pi == swapped, 1.0, 0.0).astype(BF16)

    def pick_rows(a, rows):
        @pl.loop(0, QUART // 256)
        def _(t):
            acc = jnp.zeros((TOK, 256), F32)
            for q in range(4):
                cols = pl.ds(pl.multiple_of(q * QUART + t * 256, 256), 256)
                acc += jnp.dot(pick[4 * a + q], rows[:, cols], preferred_element_type=F32)
            cols = pl.ds(pl.multiple_of(t * 256, 256), 256)
            sraw[a, :, cols] = acc.astype(BF16)
            rraw[a, 0:16, cols] = acc[0:16].astype(BF16)

    scatter = {}

    def send_raw(a):
        for k in range(1, NODES):
            part = (a, pl.ds(16 * k, 16))
            scatter[a, k] = send(sraw.at[part], rraw.at[part], dest(k))

    ld_tok.wait()
    pick_rows(0, tok)
    pl.semaphore_wait(barrier, len(partners))
    send_raw(0)
    ld_og.wait()
    pick_rows(1, og)
    send_raw(1)

    left, right = pl.ds(0, HALF), pl.ds(HALF, HALF)
    gath = {}

    def unit(u):
        return u % 2, (u // 2) * ROWS

    def spread(u):
        a, at = unit(u)
        p = u // 2
        for k in range(4 * p, 4 * p + 4):
            if k:
                scatter[a, k].wait_recv()
        rows = jnp.dot(perm[...], rraw[a, 64 * p:64 * p + 64, :], preferred_element_type=F32).astype(BF16)
        for q in range(4):
            xg[a, at:at + 16, q * QUART:(q + 1) * QUART] = rows[16 * q:16 * q + 16]
        mine = xg.at[a, pl.ds(at, 16)]
        gath[u, "u"] = send(mine, xg.at[a, pl.ds(at + 16, 16)], up)
        gath[u, "d"] = send(mine, xg.at[a, pl.ds(at + 32, 16)], down)
        gath[u, "c0"] = send(mine, xg.at[a, pl.ds(at + 64, 16)], other)

    def forward(u):
        a, at = unit(u)
        opp = pl.ds(at + 48, 16)
        gath[u, "u"].wait_recv()
        gath[u, "fu"] = send(xg.at[a, pl.ds(at + 16, 16), left], xg.at[a, opp, left], up)
        gath[u, "d"].wait_recv()
        gath[u, "fd"] = send(xg.at[a, pl.ds(at + 32, 16), right], xg.at[a, opp, right], down)
        gath[u, "c12"] = send(xg.at[a, pl.ds(at + 16, 32)], xg.at[a, pl.ds(at + 80, 32)], other)

    def opposite(u):
        a, at = unit(u)
        gath[u, "fu"].wait_recv()
        gath[u, "fd"].wait_recv()
        gath[u, "c3"] = send(xg.at[a, pl.ds(at + 48, 16)], xg.at[a, pl.ds(at + 112, 16)], other)

    back = {}

    def compute(p):
        for u in (2 * p, 2 * p + 1):
            for part in ("c0", "c12", "c3"):
                gath[u, part].wait_recv()
        at = p * ROWS
        pre = jnp.dot(xg[0, at:at + ROWS, :], wgu[...], preferred_element_type=F32)
        hidden_grad = contract_cols(xg[1, at:at + ROWS, :], wd[...])
        gate_pre, up_pre = pre[:, :FFD], pre[:, FFD:]
        logistic = jax.nn.sigmoid(gate_pre)
        silu = gate_pre * logistic
        hidden = (silu * up_pre).astype(BF16).astype(F32)
        gate_delta = hidden_grad * up_pre * logistic * (1.0 + gate_pre * (1.0 - logistic))
        up_delta = hidden_grad * silu
        part = jnp.sum(hidden * hidden_grad, axis=1, keepdims=True)
        part = jnp.broadcast_to(part, (ROWS, SCW))
        score[p] = part[0:64]
        dl[p, :, 0:FFD] = gate_delta[0:64].astype(BF16)
        dl[p, :, FFD:2 * FFD] = up_delta[0:64].astype(BF16)
        psend[p, :, 0:FFD] = gate_delta[64:128].astype(BF16)
        psend[p, :, FFD:2 * FFD] = up_delta[64:128].astype(BF16)
        psend[p, :, 2 * FFD:] = hi_lo(part[64:128])
        back[p, "c"] = send(psend.at[p], precv.at[p], other)
        dlt[0:FFD, at:at + ROWS] = gate_delta.T.astype(BF16)
        dlt[FFD:2 * FFD, at:at + ROWS] = up_delta.T.astype(BF16)
        hidt[:, at:at + ROWS] = hidden.T.astype(BF16)

    def row_grads(p):
        back[p, "c"].wait_recv()
        mine, theirs = dl[p], precv[p, :, 0:2 * FFD]
        total = score[p] + from_hi_lo(precv[p, :, 2 * FFD:])
        rgf[p, :, D:] = total[0:48]
        o3s[p, :, D:] = hi_lo(total[48:64])
        j2s[p, :, D:] = hi_lo(total[32:48])

        def tiles(lo, hi, ready):
            @pl.loop(lo, hi)
            def _(t):
                cols = pl.ds(pl.multiple_of(t * 512, 512), 512)
                grad = contract_cols(mine, wgu[cols, :]) + contract_cols(theirs, wgup[cols, :])
                rgf[p, :, cols] = grad[0:48]
                o3s[p, :, cols] = grad[48:64].astype(BF16)
                ready[p, :, cols] = grad[16:32].astype(BF16) if ready is j1s else grad[32:48].astype(BF16)

        tiles(0, 7, j1s)
        back[p, "ol"] = send(o3s.at[p, :, left], o3r.at[p, :, left], up)
        back[p, "j1l"] = send(j1s.at[p, :, left], j1r.at[p, :, left], down)
        tiles(7, 14, j2s)
        tail = pl.ds(HALF, RW - HALF)
        back[p, "or"] = send(o3s.at[p, :, tail], o3r.at[p, :, tail], down)
        back[p, "j2r"] = send(j2s.at[p, :, tail], j2r.at[p, :, tail], up)

    def merge(p):
        back[p, "ol"].wait_recv()
        j2s[p, :, 0:HALF] = (rgf[p, 32:48, 0:HALF] + o3r[p, :, 0:HALF].astype(F32)).astype(BF16)
        back[p, "j2l"] = send(j2s.at[p, :, left], j2r.at[p, :, left], up)
        back[p, "or"].wait_recv()
        j1s[p, :, HALF:D] = (rgf[p, 16:32, HALF:D] + o3r[p, :, HALF:D].astype(F32)).astype(BF16)
        j1s[p, :, D:] = hi_lo(rgf[p, 16:32, D:] + from_hi_lo(o3r[p, :, D:]))
        tail = pl.ds(HALF, RW - HALF)
        back[p, "j1r"] = send(j1s.at[p, :, tail], j1r.at[p, :, tail], down)

    def home(p):
        for part in ("j1l", "j1r", "j2l", "j2r"):
            back[p, part].wait_recv()
        for q in range(4):
            cols = slice(q * QUART, (q + 1) * QUART)
            full = rgf[p, 0:16, cols] + j1r[p, :, cols].astype(F32) + j2r[p, :, cols].astype(F32)
            fstk[16 * q:16 * q + 16, 0:QUART] = full.astype(BF16)
        total = hi_lo(rgf[p, 0:16, D:] + from_hi_lo(j1r[p, :, D:]) + from_hi_lo(j2r[p, :, D:]))
        for q in range(4):
            fstk[16 * q:16 * q + 16, QUART:] = total
        block = jnp.dot(perm[...], fstk[...], preferred_element_type=F32).astype(BF16)
        rets[64 * p:64 * p + 64, :] = block
        if p == 0:
            retr[0:16, :] = block[0:16]
        for k in range(4 * p, 4 * p + 4):
            if k:
                part = pl.ds(16 * k, 16)
                back[k] = send(rets.at[part], retr.at[part], source(k))

    outs = []

    def store(src, dst):
        copy = pltpu.make_async_copy(src, dst, lsem.at[len(local)])
        local.append(copy)
        outs.append(copy)
        copy.start()

    def weight_grads(lo, hi):
        @pl.loop(lo, hi)
        def _(t):
            cols = pl.ds(pl.multiple_of(t * 512, 512), 512)
            both = jnp.dot(dlt[...], xg[0, :, cols], preferred_element_type=F32)
            ggo[cols, :] = both[0:FFD].T.astype(BF16)
            guo[cols, :] = both[FFD:].T.astype(BF16)
            gdo[:, cols] = jnp.dot(hidt[...], xg[1, :, cols], preferred_element_type=F32).astype(BF16)

    spread(0)
    spread(1)
    ld_wg.wait()
    ld_wu.wait()
    weights = send(wgu, wgup, other)
    forward(0)
    spread(2)
    forward(1)
    opposite(0)
    spread(3)
    ld_wd.wait()
    forward(2)
    opposite(1)
    spread(4)
    compute(0)
    forward(3)
    opposite(2)
    spread(5)
    weights.wait_recv()
    row_grads(0)
    forward(4)
    opposite(3)
    spread(6)
    compute(1)
    merge(0)
    forward(5)
    opposite(4)
    spread(7)
    row_grads(1)
    home(0)
    forward(6)
    opposite(5)
    compute(2)
    merge(1)
    forward(7)
    opposite(6)
    row_grads(2)
    home(1)
    opposite(7)
    compute(3)
    merge(2)
    row_grads(3)
    home(2)
    weight_grads(0, 4)
    merge(3)
    weight_grads(4, 8)
    home(3)
    weight_grads(8, 14)
    store(ggo, gg_hbm)
    store(guo, gu_hbm)
    store(gdo, gd_hbm)
    for k in range(1, NODES):
        back[k].wait_recv()
    store(retr, ret_hbm)
    for copy in remote:
        copy.wait_send()
    for copy in outs:
        copy.wait()


def scatter_kernel(ids, gates, ret, grad, gate_grad):
    node = lax.axis_index("node")
    gx, gz = node // SIDE, node % SIDE
    target, gate = slot_targets(ids[...], gates[...])
    want, quarter = wanted(iota((TOK, TOK), 1), gx, gz)
    hit = want == target
    q = pl.program_id(0)
    chosen = jnp.where(hit & (quarter == q), 1.0, 0.0).astype(BF16)
    grad[...] = jnp.dot(chosen, ret[:, 0:QUART], preferred_element_type=F32).astype(BF16)

    @pl.when(q == 0)
    def _():
        pair = jnp.dot(chosen, ret[:, QUART:], preferred_element_type=F32)
        lane = iota(pair.shape, 1)
        total = jnp.sum(jnp.where((lane & 63) == 0, pair, 0.0), axis=1, keepdims=True)
        scaled = total / jnp.where(gate > 0.0, gate, 1.0)
        gate_grad[...] = jnp.where(ids[...] < NODES, scaled, 0.0)


def body(tokens, out_grad, route_ids, route_gates, w_gate, w_up, w_down):
    any_space = pl.BlockSpec(memory_space=pl.ANY)
    in_vmem = pl.BlockSpec(memory_space=pltpu.VMEM)
    copies = 30 + 8 * 7 + 4 + 4 * 6 + 15 + 1
    ret, gg, gu, gd = pl.pallas_call(
        exchange_kernel,
        out_shape=(
            jax.ShapeDtypeStruct((TOK, QUART + SCW), BF16),
            jax.ShapeDtypeStruct((D, FFD), BF16),
            jax.ShapeDtypeStruct((D, FFD), BF16),
            jax.ShapeDtypeStruct((FFD, D), BF16),
        ),
        in_specs=[in_vmem, in_vmem] + [any_space] * 5,
        out_specs=(any_space,) * 4,
        scratch_shapes=[
            pltpu.VMEM((TOK, D), BF16),
            pltpu.VMEM((TOK, D), BF16),
            pltpu.VMEM((8, TOK, TOK), BF16),
            pltpu.VMEM((2, TOK, QUART), BF16),
            pltpu.VMEM((2, TOK, QUART), BF16),
            pltpu.VMEM((2, PH * ROWS, D), BF16),
            pltpu.VMEM((D, 2 * FFD), BF16),
            pltpu.VMEM((D, 2 * FFD), BF16),
            pltpu.VMEM((FFD, D), BF16),
            pltpu.VMEM((PH, 64, 2 * FFD), BF16),
            pltpu.VMEM((2 * FFD, PH * ROWS), BF16),
            pltpu.VMEM((FFD, PH * ROWS), BF16),
            pltpu.VMEM((PH, 64, SCW), F32),
            pltpu.VMEM((PH, 64, 2 * FFD + SCW), BF16),
            pltpu.VMEM((PH, 64, 2 * FFD + SCW), BF16),
            pltpu.VMEM((PH, 48, RW), F32),
            pltpu.VMEM((PH, 16, RW), BF16),
            pltpu.VMEM((PH, 16, RW), BF16),
            pltpu.VMEM((PH, 16, RW), BF16),
            pltpu.VMEM((PH, 16, RW), BF16),
            pltpu.VMEM((PH, 16, RW), BF16),
            pltpu.VMEM((PH, 16, RW), BF16),
            pltpu.VMEM((64, QUART + SCW), BF16),
            pltpu.VMEM((TOK, QUART + SCW), BF16),
            pltpu.VMEM((TOK, QUART + SCW), BF16),
            pltpu.VMEM((D, FFD), BF16),
            pltpu.VMEM((D, FFD), BF16),
            pltpu.VMEM((FFD, D), BF16),
            pltpu.VMEM((64, 64), BF16),
            pltpu.SemaphoreType.DMA((copies,)),
            pltpu.SemaphoreType.DMA((copies,)),
            pltpu.SemaphoreType.DMA((9,)),
        ],
        compiler_params=pltpu.CompilerParams(
            collective_id=0, has_side_effects=True, vmem_limit_bytes=60 * 2**20
        ),
        cost_estimate=pl.CostEstimate(
            flops=8 * 10**9, bytes_accessed=20 * 10**6, transcendentals=65536
        ),
        name="exchange",
    )(route_ids, route_gates, tokens, out_grad, w_gate[0], w_up[0], w_down[0])
    token_grad, gate_grad = pl.pallas_call(
        scatter_kernel,
        grid=(4,),
        out_shape=(
            jax.ShapeDtypeStruct((TOK, D), BF16),
            jax.ShapeDtypeStruct((TOK, 8), F32),
        ),
        in_specs=[
            pl.BlockSpec((TOK, 8), lambda q: (0, 0)),
            pl.BlockSpec((TOK, 8), lambda q: (0, 0)),
            pl.BlockSpec((TOK, QUART + SCW), lambda q: (0, 0)),
        ],
        out_specs=(
            pl.BlockSpec((TOK, QUART), lambda q: (0, q)),
            pl.BlockSpec((TOK, 8), lambda q: (0, 0)),
        ),
        compiler_params=pltpu.CompilerParams(vmem_limit_bytes=16 * 2**20),
        name="scatter",
    )(route_ids, route_gates, ret)
    return token_grad, gate_grad, gg[None], gu[None], gd[None]


def solution(mesh):
    return jax.shard_map(
        body,
        mesh=mesh,
        in_specs=(
            P(("node", "local"), None),
            P(("node", "local"), None),
            P(("node", "local"), None),
            P(("node", "local"), None),
            P("node", None, "local"),
            P("node", None, "local"),
            P("node", "local", None),
        ),
        out_specs=(
            P(("node", "local"), None),
            P(("node", "local"), None),
            P("node", None, "local"),
            P("node", None, "local"),
            P("node", "local", None),
        ),
        check_vma=False,
    )
```

time: 561 us -> 147 us (0.26)
  the two profiles are of different devices: /device:TPU:114 before, /device:TPU:0 now
where the time goes in v1:
time: 147 us
  Pallas kernels  135 us (92%)
  local copies, waits for them, and re-layouts  11.1 us (8%)
    pallas_call x1, Pallas kernels, body(): pl.pallas_call(exchange_kernel, out_shape=(jax.ShapeDtypeStruct((TOK, QUA...  131 us
    unnamed x16, local copies, waits for them, and re-layouts  11.1 us
    pallas_call x1, Pallas kernels, body(): pl.pallas_call(scatter_kernel, grid=(4,), out_shape=(jax.ShapeDtypeStruct...  4.35 us

profile of v1, /device:TPU:0, one launch (start us, length us, event | category | flops | bytes accessed | tf_op | source)
XLA Modules:
  0.0 147.2 jit_solution(10792341875706135264)
XLA Ops:
  0.6 1.4 copy.15.gates
  2.1 1.5 %copy.14.ids = s32[256,8]{1,0:T(8,128)} copy(s32[256,8]{0,1:T(8,128)} %param.9) | data formatting | bytes 16384 | tf_op args[2]
  3.5 0.0 copy-start.1
  3.5 0.0 copy-start.2
  3.5 131.0 %exchange.1 = (bf16[256,1920]{1,0:T(8,128)(2,1)}, bf16[7168,128]{1,0:T(8,128)(2,1)}, bf16[7168,128]{1,0:T(8,128)(2,1)}, bf16[128,7168]{1,0:T(8,128)(2,1)}) custom-call(s32[256,8]{1,0:T(8,128)} %copy.14.ids, bf16[256,8]{1,0:T(8,128)(2,1)} %copy.15.gates, bf16[256,7168]{1,0:T(8,128)(2,1)} %tok_hbm.1, bf16[256,7168]{1,0:T(8,128)(2,1)} %og_hbm.1, ...), custom_call_target="tpu_custom_call" | custom-call | flops 8000000000 | bytes 20000000 | tf_op jit(solution)/shard_map/exchange/pallas_call | solution.py:387
  134.6 0.0 copy-done.1
  134.6 0.0 copy-done.2
  134.6 0.0 copy-start
  134.6 1.2 copy-done
  135.8 4.4 %scatter.1 = (bf16[256,7168]{1,0:T(8,128)(2,1)}, f32[256,8]{1,0:T(8,128)S(1)}) custom-call(s32[256,8]{1,0:T(8,128)S(1)} %copy-done.1, bf16[256,8]{1,0:T(8,128)(2,1)S(1)} %copy-done.2, bf16[256,1920]{1,0:T(8,128)(2,1)S(1)} %copy-done), custom_call_target="tpu_custom_call" | custom-call | tf_op jit(solution)/shard_map/scatter/pallas_call | solution.py:439
  140.1 0.7 copy.16
  140.8 0.0 copy-start.4
  140.8 3.0 %copy.20 = bf16[1,7168,128]{2,1,0:T(8,128)(2,1)} copy(bf16[1,7168,128]{2,1,0:T(8,128)(2,1)} %bitcast.8) | data formatting | bytes 3670016
  143.8 0.0 copy-done.4
  143.8 0.0 copy-start.3
  143.8 1.2 copy.21
  145.0 0.9 copy-done.3
  145.9 1.2 copy.22
Async XLA Ops:
  3.5 131.0 %copy-start.1 = (s32[256,8]{1,0:T(8,128)S(1)}, s32[256,8]{1,0:T(8,128)}, u32[]{:S(2)}) copy-start(s32[256,8]{1,0:T(8,128)} %copy.14.ids) | copy-start | bytes 24580
  3.5 131.0 %copy-start.2 = (bf16[256,8]{1,0:T(8,128)(2,1)S(1)}, bf16[256,8]{1,0:T(8,128)(2,1)}, u32[]{:S(2)}) copy-start(bf16[256,8]{1,0:T(8,128)(2,1)} %copy.15.gates) | copy-start | bytes 12292
  134.6 1.2 copy-start
  140.8 3.0 %copy-start.4 = (bf16[7168,128]{1,0:T(8,128)(2,1)S(1)}, bf16[7168,128]{1,0:T(8,128)(2,1)}, u32[]{:S(2)}) copy-start(bf16[7168,128]{1,0:T(8,128)(2,1)} %get-tuple-element.15) | copy-start | bytes 5505028
  143.8 2.2 %copy-start.3 = (bf16[128,7168]{1,0:T(8,128)(2,1)S(1)}, bf16[128,7168]{1,0:T(8,128)(2,1)}, u32[]{:S(2)}) copy-start(bf16[128,7168]{1,0:T(8,128)(2,1)} %get-tuple-element.16) | copy-start | bytes 5505028

commit v2 on v1

v2 whole, which is shorter than its diff:
```python
import functools

import jax
import jax.numpy as jnp
from jax import lax
from jax.experimental import pallas as pl
from jax.experimental.pallas import tpu as pltpu
from jax.sharding import PartitionSpec as P

MESH = pl.DeviceIdType.MESH
F32 = jnp.float32
BF16 = jnp.bfloat16

CAP = 4
TOK = 256
D = 7168
HALF = D // 2
QUART = D // 4
FFD = 128
NODES = 16
SIDE = 4
SCW = 128
RW = D + SCW
PH = 4
OFFSETS = (
    (0, 0), (1, 1), (3, 3), (1, 3), (3, 1), (0, 2), (2, 0), (2, 2),
    (1, 2), (3, 2), (2, 1), (2, 3), (0, 1), (0, 3), (1, 0), (3, 0),
)


def two_bits(values):
    word = sum(v << (2 * i) for i, v in enumerate(values))
    return word - 2**32 if word >= 2**31 else word


DX_BITS = two_bits([dx for dx, _ in OFFSETS])
DZ_BITS = two_bits([dz for _, dz in OFFSETS])
ROWS = 128


def iota(shape, dim):
    return lax.broadcasted_iota(jnp.int32, shape, dim)


def slot_targets(ids, gates):
    held = ids < NODES
    expert = jnp.sum(jnp.where(held, ids, 0).astype(F32), axis=0, keepdims=True)
    inside = jnp.sum(jnp.where(held, 1.0, 0.0), axis=0, keepdims=True) > 0.5
    gate = jnp.sum(jnp.where(held, gates.astype(F32), 0.0), axis=0, keepdims=True)
    row = iota((NODES, TOK), 0).astype(F32)
    one_hot = jnp.where((row == expert) & inside, 1.0, 0.0)
    before = jnp.where(iota((TOK, TOK), 0) < iota((TOK, TOK), 1), 1.0, 0.0)
    ranks = jnp.dot(one_hot.astype(BF16), before.astype(BF16), preferred_element_type=F32)
    rank = jnp.sum(ranks * one_hot, axis=0, keepdims=True)
    target = jnp.where(inside, expert * CAP + rank, -1.0)
    return target, gate


def wanted(block, gx, gz):
    k = block >> 4
    dx = lax.shift_right_logical(jnp.full(k.shape, DX_BITS, jnp.int32), 2 * k) & 3
    dz = lax.shift_right_logical(jnp.full(k.shape, DZ_BITS, jnp.int32), 2 * k) & 3
    node = ((gx - dx) & 3) * SIDE + ((gz - dz) & 3)
    return (node * CAP + (block & 3)).astype(F32), (block >> 2) & 3


def hi_lo(score):
    hi = score.astype(BF16).astype(F32)
    lane = iota(score.shape, 1)
    return jnp.where(lane < 64, hi, score - hi).astype(BF16)


def from_hi_lo(pair):
    wide = pair.astype(F32)
    return wide + pltpu.roll(wide, 64, 1)


def contract_cols(left, right):
    return lax.dot_general(left, right, (((1,), (1,)), ((), ())), preferred_element_type=F32)


def exchange_kernel(
    ids_hbm, gates_hbm, tok_hbm, og_hbm, wg_hbm, wu_hbm, wd_hbm,
    retr, ggo, guo, gdo,
    ids, gates, tok, og, pick, sraw, rraw, rx, xg, wgu, wgup, wd,
    dl, dlt, hidt, score, psend, precv,
    rgf, o3s, o3r, j1s, j1r, j2s, j2r, fstk, rets, perm, pre_ref,
    ssem, rsem, lsem,
):
    node = lax.axis_index("node")
    loc = lax.axis_index("local")
    gx, gz = node // SIDE, node % SIDE
    y, c = loc // 2, loc % 2
    up = (node, ((y + 1) % 4) * 2 + c)
    down = (node, ((y + 3) % 4) * 2 + c)
    other = (node, y * 2 + 1 - c)

    def dest(k):
        dx, dz = OFFSETS[k]
        return (((gx + 4 - dx) % 4) * SIDE + (gz + 4 - dz) % 4, loc)

    def source(k):
        dx, dz = OFFSETS[k]
        return (((gx + dx) % 4) * SIDE + (gz + dz) % 4, loc)

    barrier = pltpu.get_barrier_semaphore()
    partners = [up, down, other] + [dest(k) for k in range(1, NODES)]
    for who in partners:
        pl.semaphore_signal(barrier, inc=1, device_id=who, device_id_type=MESH)

    local = []

    def load(src, dst):
        copy = pltpu.make_async_copy(src, dst, lsem.at[len(local)])
        local.append(copy)
        copy.start()
        return copy

    ld_ids = load(ids_hbm, ids)
    ld_gates = load(gates_hbm, gates)
    ld_tok = load(tok_hbm, tok)
    ld_og = load(og_hbm, og)

    remote = []

    def send(src, dst, who):
        i = len(remote)
        copy = pltpu.make_async_remote_copy(
            src_ref=src, dst_ref=dst, send_sem=ssem.at[i], recv_sem=rsem.at[i],
            device_id=who, device_id_type=MESH,
        )
        remote.append(copy)
        copy.start()
        return copy

    ld_ids.wait()
    ld_gates.wait()
    target, gate = slot_targets(ids[...], gates[...])
    want, quarter = wanted(iota((TOK, TOK), 0), gx, gz)
    hit = want == target
    for q in range(4):
        chosen = hit & (quarter == q)
        pick[q] = jnp.where(chosen, 1.0, 0.0).astype(BF16)
        pick[4 + q] = jnp.where(chosen, gate, 0.0).astype(BF16)
    pi, pj = iota((64, 64), 0), iota((64, 64), 1)
    swapped = ((pj >> 2) & 3) * 16 + (pj >> 4) * 4 + (pj & 3)
    perm[...] = jnp.where(pi == swapped, 1.0, 0.0).astype(BF16)

    def pick_rows(a, rows, lo, hi):
        @pl.loop(0, QUART // 256)
        def _(t):
            acc = jnp.zeros((hi - lo, 256), F32)
            for q in range(4):
                cols = pl.ds(pl.multiple_of(q * QUART + t * 256, 256), 256)
                acc += jnp.dot(pick[4 * a + q, lo:hi, :], rows[:, cols], preferred_element_type=F32)
            cols = pl.ds(pl.multiple_of(t * 256, 256), 256)
            sraw[a, lo:hi, cols] = acc.astype(BF16)
            if lo == 0:
                rx[a, 0, 0:16, cols] = acc[0:16].astype(BF16)

    scatter = {}

    def send_part(u):
        a, p = u % 2, u // 2
        for k in range(4 * p, 4 * p + 4):
            if k:
                part = pl.ds(16 * k, 16)
                land = rraw.at[a, part] if p else rx.at[a, 0, part]
                scatter[a, k] = send(sraw.at[a, part], land, dest(k))

    gath = {}

    def own_block(a, name, rows):
        block = rx.at[a, 0, rows]
        gath[a, "u" + name] = send(block, rx.at[a, 1, rows], up)
        gath[a, "d" + name] = send(block, rx.at[a, 2, rows], down)
        gath[a, "c0" + name] = send(block, rx.at[a, 4, rows], other)

    def rest(a):
        for k in range(1, 4):
            scatter[a, k].wait_recv()
        own_block(a, "", pl.ds(16, 48))

    ld_tok.wait()
    pick_rows(0, tok, 0, 64)
    pl.semaphore_wait(barrier, len(partners))
    own_block(0, "first", pl.ds(0, 16))
    send_part(0)
    ld_og.wait()
    ld_wg = load(wg_hbm, wgu.at[:, pl.ds(0, FFD)])
    ld_wu = load(wu_hbm, wgu.at[:, pl.ds(FFD, FFD)])
    ld_wd = load(wd_hbm, wd)
    pick_rows(1, og, 0, 64)
    own_block(1, "first", pl.ds(0, 16))
    send_part(1)
    pick_rows(0, tok, 64, TOK)

    left, right = pl.ds(0, HALF), pl.ds(HALF, HALF)

    def unit(u):
        return u % 2, (u // 2) * ROWS

    def spread(u):
        a, at = unit(u)
        p = u // 2
        for k in range(4 * p, 4 * p + 4):
            if k:
                scatter[a, k].wait_recv()
        rows = jnp.dot(perm[...], rraw[a, 64 * p:64 * p + 64, :], preferred_element_type=F32).astype(BF16)
        for q in range(4):
            xg[a, at:at + 16, q * QUART:(q + 1) * QUART] = rows[16 * q:16 * q + 16]
        mine = xg.at[a, pl.ds(at, 16)]
        gath[u, "u"] = send(mine, xg.at[a, pl.ds(at + 16, 16)], up)
        gath[u, "d"] = send(mine, xg.at[a, pl.ds(at + 32, 16)], down)
        gath[u, "c0"] = send(mine, xg.at[a, pl.ds(at + 64, 16)], other)

    def forward(u):
        a, at = unit(u)
        if u < 2:
            near, far = pl.ds(0, QUART // 2), pl.ds(QUART // 2, QUART // 2)
            gath[u, "ufirst"].wait_recv()
            gath[u, "u"].wait_recv()
            gath[u, "fu"] = send(rx.at[a, 1, :, near], rx.at[a, 3, :, near], up)
            gath[u, "dfirst"].wait_recv()
            gath[u, "d"].wait_recv()
            gath[u, "fd"] = send(rx.at[a, 2, :, far], rx.at[a, 3, :, far], down)
            gath[u, "c12"] = send(rx.at[a, pl.ds(1, 2)], rx.at[a, pl.ds(5, 2)], other)
            return
        opp = pl.ds(at + 48, 16)
        gath[u, "u"].wait_recv()
        gath[u, "fu"] = send(xg.at[a, pl.ds(at + 16, 16), left], xg.at[a, opp, left], up)
        gath[u, "d"].wait_recv()
        gath[u, "fd"] = send(xg.at[a, pl.ds(at + 32, 16), right], xg.at[a, opp, right], down)
        gath[u, "c12"] = send(xg.at[a, pl.ds(at + 16, 32)], xg.at[a, pl.ds(at + 80, 32)], other)

    def opposite(u):
        a, at = unit(u)
        gath[u, "fu"].wait_recv()
        gath[u, "fd"].wait_recv()
        if u < 2:
            gath[u, "c3"] = send(rx.at[a, 3], rx.at[a, 7], other)
            return
        gath[u, "c3"] = send(xg.at[a, pl.ds(at + 48, 16)], xg.at[a, pl.ds(at + 112, 16)], other)

    back = {}

    def arrived(u):
        a, at = unit(u)
        for part in ("c0", "c12", "c3"):
            gath[u, part].wait_recv()
        if u < 2:
            gath[u, "c0first"].wait_recv()

            @pl.loop(0, 8)
            def _(b):
                rows = jnp.dot(perm[...], rx[a, b], preferred_element_type=F32).astype(BF16)
                to = pl.ds(pl.multiple_of(b * 16, 16), 16)
                for q in range(4):
                    xg[a, to, q * QUART:(q + 1) * QUART] = rows[16 * q:16 * q + 16]

    def project(p):
        arrived(2 * p)
        at = p * ROWS
        pre_ref[...] = jnp.dot(xg[0, at:at + ROWS, :], wgu[...], preferred_element_type=F32)

    def compute(p):
        arrived(2 * p + 1)
        at = p * ROWS
        pre = pre_ref[...]
        hidden_grad = contract_cols(xg[1, at:at + ROWS, :], wd[...])
        gate_pre, up_pre = pre[:, :FFD], pre[:, FFD:]
        logistic = jax.nn.sigmoid(gate_pre)
        silu = gate_pre * logistic
        hidden = (silu * up_pre).astype(BF16).astype(F32)
        gate_delta = hidden_grad * up_pre * logistic * (1.0 + gate_pre * (1.0 - logistic))
        up_delta = hidden_grad * silu
        part = jnp.sum(hidden * hidden_grad, axis=1, keepdims=True)
        part = jnp.broadcast_to(part, (ROWS, SCW))
        score[p] = part[0:64]
        dl[p, :, 0:FFD] = gate_delta[0:64].astype(BF16)
        dl[p, :, FFD:2 * FFD] = up_delta[0:64].astype(BF16)
        psend[p, :, 0:FFD] = gate_delta[64:128].astype(BF16)
        psend[p, :, FFD:2 * FFD] = up_delta[64:128].astype(BF16)
        psend[p, :, 2 * FFD:] = hi_lo(part[64:128])
        back[p, "c"] = send(psend.at[p], precv.at[p], other)
        dlt[0:FFD, at:at + ROWS] = gate_delta.T.astype(BF16)
        dlt[FFD:2 * FFD, at:at + ROWS] = up_delta.T.astype(BF16)
        hidt[:, at:at + ROWS] = hidden.T.astype(BF16)

    tail = pl.ds(HALF, RW - HALF)

    def row_tiles(p, lo, hi, ready):
        mine, theirs = dl[p], precv[p, :, 0:2 * FFD]

        @pl.loop(lo, hi)
        def _(t):
            cols = pl.ds(pl.multiple_of(t * 512, 512), 512)
            grad = contract_cols(mine, wgu[cols, :]) + contract_cols(theirs, wgup[cols, :])
            rgf[p % 2, :, cols] = grad[0:48]
            o3s[p, :, cols] = grad[48:64].astype(BF16)
            ready[p, :, cols] = grad[16:32].astype(BF16) if ready is j1s else grad[32:48].astype(BF16)

    def row_left(p):
        back[p, "c"].wait_recv()
        total = score[p] + from_hi_lo(precv[p, :, 2 * FFD:])
        rgf[p % 2, :, D:] = total[0:48]
        o3s[p, :, D:] = hi_lo(total[48:64])
        j2s[p, :, D:] = hi_lo(total[32:48])
        row_tiles(p, 0, 7, j1s)

    def row_right(p):
        row_tiles(p, 7, 14, j2s)

    def send_left(p):
        back[p, "ol"] = send(o3s.at[p, :, left], o3r.at[p, :, left], up)
        back[p, "j1l"] = send(j1s.at[p, :, left], j1r.at[p, :, left], down)

    def send_right(p):
        back[p, "or"] = send(o3s.at[p, :, tail], o3r.at[p, :, tail], down)
        back[p, "j2r"] = send(j2s.at[p, :, tail], j2r.at[p, :, tail], up)

    def row_grads(p):
        row_left(p)
        send_left(p)
        row_right(p)
        send_right(p)

    def merge(p):
        back[p, "ol"].wait_recv()
        j2s[p, :, 0:HALF] = (rgf[p % 2, 32:48, 0:HALF] + o3r[p, :, 0:HALF].astype(F32)).astype(BF16)
        back[p, "j2l"] = send(j2s.at[p, :, left], j2r.at[p, :, left], up)
        back[p, "or"].wait_recv()
        j1s[p, :, HALF:D] = (rgf[p % 2, 16:32, HALF:D] + o3r[p, :, HALF:D].astype(F32)).astype(BF16)
        j1s[p, :, D:] = hi_lo(rgf[p % 2, 16:32, D:] + from_hi_lo(o3r[p, :, D:]))
        back[p, "j1r"] = send(j1s.at[p, :, tail], j1r.at[p, :, tail], down)

    def home(p):
        for part in ("j1l", "j1r", "j2l", "j2r"):
            back[p, part].wait_recv()
        for q in range(4):
            cols = slice(q * QUART, (q + 1) * QUART)
            full = rgf[p % 2, 0:16, cols] + j1r[p, :, cols].astype(F32) + j2r[p, :, cols].astype(F32)
            fstk[16 * q:16 * q + 16, 0:QUART] = full.astype(BF16)
        total = hi_lo(rgf[p % 2, 0:16, D:] + from_hi_lo(j1r[p, :, D:]) + from_hi_lo(j2r[p, :, D:]))
        for q in range(4):
            fstk[16 * q:16 * q + 16, QUART:] = total
        block = jnp.dot(perm[...], fstk[...], preferred_element_type=F32).astype(BF16)
        rets[64 * p:64 * p + 64, :] = block
        if p == 0:
            retr[0:16, :] = block[0:16]
        for k in range(4 * p, 4 * p + 4):
            if k:
                part = pl.ds(16 * k, 16)
                back[k] = send(rets.at[part], retr.at[part], source(k))

    def weight_grads(lo, hi):
        @pl.loop(lo, hi)
        def _(t):
            cols = pl.ds(pl.multiple_of(t * 512, 512), 512)
            both = jnp.dot(dlt[...], xg[0, :, cols], preferred_element_type=F32)
            ggo[cols, :] = both[0:FFD].T.astype(BF16)
            guo[cols, :] = both[FFD:].T.astype(BF16)
            gdo[:, cols] = jnp.dot(hidt[...], xg[1, :, cols], preferred_element_type=F32).astype(BF16)

    send_part(2)
    rest(0)
    pick_rows(1, og, 64, TOK)
    send_part(3)
    rest(1)
    ld_wg.wait()
    ld_wu.wait()
    ld_wd.wait()
    forward(0)
    spread(2)
    send_part(4)
    forward(1)
    opposite(0)
    spread(3)
    send_part(5)
    weights = send(wgu, wgup, other)
    forward(2)
    opposite(1)
    project(0)
    compute(0)
    spread(4)
    send_part(6)
    forward(3)
    opposite(2)
    spread(5)
    send_part(7)
    weights.wait_recv()
    row_grads(0)
    forward(4)
    opposite(3)
    project(1)
    compute(1)
    spread(6)
    merge(0)
    forward(5)
    opposite(4)
    spread(7)
    row_grads(1)
    home(0)
    forward(6)
    opposite(5)
    project(2)
    compute(2)
    forward(7)
    opposite(6)
    row_left(2)
    row_right(2)
    project(3)
    merge(1)
    opposite(7)
    send_left(2)
    send_right(2)
    compute(3)
    home(1)
    row_left(3)
    send_left(3)
    row_right(3)
    send_right(3)
    merge(2)
    home(2)
    merge(3)
    weight_grads(0, 14)
    home(3)
    for k in range(1, NODES):
        back[k].wait_recv()
    for copy in remote:
        copy.wait_send()


def scatter_kernel(ids, gates, ret, grad_hbm, gate_grad, grad, sem):
    copies = []

    def start(src, dst):
        copy = pltpu.make_async_copy(src, dst, sem.at[len(copies)])
        copies.append(copy)
        copy.start()

    node = lax.axis_index("node")
    gx, gz = node // SIDE, node % SIDE
    target, gate = slot_targets(ids[...], gates[...])
    eye = iota((TOK, TOK), 0) == iota((TOK, TOK), 1)
    target_col = jnp.sum(jnp.where(eye, target, 0.0), axis=1, keepdims=True)
    want, quarter = wanted(iota((TOK, TOK), 1), gx, gz)
    hit = want == target_col
    for q in range(4):
        chosen = jnp.where(hit & (quarter == q), 1.0, 0.0).astype(BF16)
        cols = pl.ds(q * QUART, QUART)
        grad[:, cols] = jnp.dot(chosen, ret[:, 0:QUART], preferred_element_type=F32).astype(BF16)
        start(grad.at[:, cols], grad_hbm.at[:, cols])
        if q == 0:
            pair = jnp.dot(chosen, ret[:, QUART:], preferred_element_type=F32)
            total = jnp.sum(jnp.where((iota(pair.shape, 1) & 63) == 0, pair, 0.0), axis=1, keepdims=True)
            total = jnp.sum(jnp.where(eye, total, 0.0), axis=0, keepdims=True)
            scaled = total / jnp.where(gate > 0.0, gate, 1.0)
            gate_grad[...] = jnp.where(ids[...] < NODES, scaled, 0.0)
    for copy in copies:
        copy.wait()


def body(tokens, out_grad, route_ids, route_gates, w_gate, w_up, w_down):
    any_space = pl.BlockSpec(memory_space=pl.ANY)
    in_vmem = pl.BlockSpec(memory_space=pltpu.VMEM)
    ids, gates = route_ids.T, route_gates.T
    copies = 30 + 8 * 7 + 6 + 4 + 4 * 6 + 15 + 1
    ret, gg, gu, gd = pl.pallas_call(
        exchange_kernel,
        out_shape=(
            pltpu.VMEM((TOK, QUART + SCW), BF16),
            pltpu.VMEM((D, FFD), BF16),
            pltpu.VMEM((D, FFD), BF16),
            pltpu.VMEM((FFD, D), BF16),
        ),
        in_specs=[any_space] * 7,
        out_specs=(in_vmem,) * 4,
        scratch_shapes=[
            pltpu.VMEM((8, TOK), jnp.int32),
            pltpu.VMEM((8, TOK), BF16),
            pltpu.VMEM((TOK, D), BF16),
            pltpu.VMEM((TOK, D), BF16),
            pltpu.VMEM((8, TOK, TOK), BF16),
            pltpu.VMEM((2, TOK, QUART), BF16),
            pltpu.VMEM((2, TOK, QUART), BF16),
            pltpu.VMEM((2, 8, 64, QUART), BF16),
            pltpu.VMEM((2, PH * ROWS, D), BF16),
            pltpu.VMEM((D, 2 * FFD), BF16),
            pltpu.VMEM((D, 2 * FFD), BF16),
            pltpu.VMEM((FFD, D), BF16),
            pltpu.VMEM((PH, 64, 2 * FFD), BF16),
            pltpu.VMEM((2 * FFD, PH * ROWS), BF16),
            pltpu.VMEM((FFD, PH * ROWS), BF16),
            pltpu.VMEM((PH, 64, SCW), F32),
            pltpu.VMEM((PH, 64, 2 * FFD + SCW), BF16),
            pltpu.VMEM((PH, 64, 2 * FFD + SCW), BF16),
            pltpu.VMEM((2, 48, RW), F32),
            pltpu.VMEM((PH, 16, RW), BF16),
            pltpu.VMEM((PH, 16, RW), BF16),
            pltpu.VMEM((PH, 16, RW), BF16),
            pltpu.VMEM((PH, 16, RW), BF16),
            pltpu.VMEM((PH, 16, RW), BF16),
            pltpu.VMEM((PH, 16, RW), BF16),
            pltpu.VMEM((64, QUART + SCW), BF16),
            pltpu.VMEM((TOK, QUART + SCW), BF16),
            pltpu.VMEM((64, 64), BF16),
            pltpu.VMEM((ROWS, 2 * FFD), F32),
            pltpu.SemaphoreType.DMA((copies,)),
            pltpu.SemaphoreType.DMA((copies,)),
            pltpu.SemaphoreType.DMA((9,)),
        ],
        compiler_params=pltpu.CompilerParams(
            collective_id=0, has_side_effects=True, vmem_limit_bytes=50 * 2**20
        ),
        cost_estimate=pl.CostEstimate(
            flops=8 * 10**9, bytes_accessed=20 * 10**6, transcendentals=65536
        ),
        name="exchange",
    )(ids, gates, tokens, out_grad, w_gate[0], w_up[0], w_down[0])
    token_grad, gate_grad = pl.pallas_call(
        scatter_kernel,
        out_shape=(
            jax.ShapeDtypeStruct((TOK, D), BF16),
            jax.ShapeDtypeStruct((8, TOK), F32),
        ),
        in_specs=[in_vmem] * 3,
        out_specs=(any_space, in_vmem),
        scratch_shapes=[
            pltpu.VMEM((TOK, D), BF16),
            pltpu.SemaphoreType.DMA((4,)),
        ],
        compiler_params=pltpu.CompilerParams(vmem_limit_bytes=16 * 2**20),
        name="scatter",
    )(ids, gates, pltpu.with_memory_space_constraint(ret, pltpu.VMEM))
    return token_grad, gate_grad.T, gg[None], gu[None], gd[None]


def solution(mesh):
    return jax.shard_map(
        body,
        mesh=mesh,
        in_specs=(
            P(("node", "local"), None),
            P(("node", "local"), None),
            P(("node", "local"), None),
            P(("node", "local"), None),
            P("node", None, "local"),
            P("node", None, "local"),
            P("node", "local", None),
        ),
        out_specs=(
            P(("node", "local"), None),
            P(("node", "local"), None),
            P("node", None, "local"),
            P("node", None, "local"),
            P("node", "local", None),
        ),
        check_vma=False,
    )
```

time: 147 us -> 127 us (0.86)
  Pallas kernels: 135 us -> 122 us
  local copies, waits for them, and re-layouts: 11.1 us -> 3.69 us
    pallas_call x2, Pallas kernels: 135 us -> 122 us  [the longest x1 119 us: body(): pl.pallas_call(exchange_kernel, out_shape=(pltpu.VMEM((TOK, QUART + SCW),...]
    unnamed x16 -> x7, local copies, waits for them, and re-layouts: 11.1 us -> 3.69 us
where the time goes in v2:
time: 127 us
  Pallas kernels  122 us (96%)
  local copies, waits for them, and re-layouts  3.69 us (3%)
    pallas_call x1, Pallas kernels, body(): pl.pallas_call(exchange_kernel, out_shape=(pltpu.VMEM((TOK, QUART + SCW),...  119 us
    unnamed x7, local copies, waits for them, and re-layouts  3.69 us
    pallas_call x1, Pallas kernels, body(): pl.pallas_call(scatter_kernel, out_shape=(jax.ShapeDtypeStruct((TOK, D),...  3.09 us

profile of v2, /device:TPU:0, one launch (start us, length us, event | category | flops | bytes accessed | tf_op | source)
XLA Modules:
  0.0 126.6 jit_solution(16564690159170021995)
XLA Ops:
  0.6 119.2 %exchange.1 = (bf16[256,1920]{1,0:T(8,128)(2,1)S(1)}, bf16[7168,128]{1,0:T(8,128)(2,1)S(1)}, bf16[7168,128]{1,0:T(8,128)(2,1)S(1)}, bf16[128,7168]{1,0:T(8,128)(2,1)S(1)}) custom-call(s32[8,256]{1,0:T(8,128)} %bitcast.12, bf16[8,256]{1,0:T(8,128)(2,1)} %bitcast.14, bf16[256,7168]{1,0:T(8,128)(2,1)} %tok_hbm.1, bf16[256,7168]{1,0:T(8,128)(2,1)} %og_hbm.1, ...), custom_call_target="tpu_custom_call" | custom-call | flops 8000000000 | bytes 20000000 | tf_op jit(solution)/shard_map/exchange/pallas_call | solution.py:469
  119.9 1.2 copy.15
  121.1 1.2 copy.16
  122.3 0.0 copy-start
  122.3 0.0 copy-start.1
  122.3 1.2 copy.17
  123.5 0.0 copy-done
  123.5 0.0 copy-done.1
  123.6 3.1 %scatter.1 = (bf16[256,7168]{1,0:T(8,128)(2,1)}, f32[8,256]{1,0:T(8,128)}) custom-call(s32[8,256]{1,0:T(8,128)S(1)} %bitcast.13, bf16[8,256]{1,0:T(8,128)(2,1)S(1)} %bitcast.15, bf16[256,1920]{1,0:T(8,128)(2,1)S(1)} %get-tuple-element.11.ret), custom_call_target="tpu_custom_call" | custom-call | tf_op jit(solution)/shard_map/scatter/pallas_call | solution.py:521
Async XLA Ops:
  122.3 1.2 copy-start
  122.3 1.2 copy-start.1

commit v3 on v2

--- a/solution.py
+++ b/solution.py
@@ -119,7 +119,6 @@
     ld_ids = load(ids_hbm, ids)
     ld_gates = load(gates_hbm, gates)
     ld_tok = load(tok_hbm, tok)
-    ld_og = load(og_hbm, og)
 
     remote = []
 
@@ -182,6 +181,7 @@
         own_block(a, "", pl.ds(16, 48))
 
     ld_tok.wait()
+    ld_og = load(og_hbm, og)
     pick_rows(0, tok, 0, 64)
     pl.semaphore_wait(barrier, len(partners))
     own_block(0, "first", pl.ds(0, 16))
@@ -276,13 +276,13 @@
         up_delta = hidden_grad * silu
         part = jnp.sum(hidden * hidden_grad, axis=1, keepdims=True)
         part = jnp.broadcast_to(part, (ROWS, SCW))
-        score[p] = part[0:64]
-        dl[p, :, 0:FFD] = gate_delta[0:64].astype(BF16)
-        dl[p, :, FFD:2 * FFD] = up_delta[0:64].astype(BF16)
         psend[p, :, 0:FFD] = gate_delta[64:128].astype(BF16)
         psend[p, :, FFD:2 * FFD] = up_delta[64:128].astype(BF16)
         psend[p, :, 2 * FFD:] = hi_lo(part[64:128])
         back[p, "c"] = send(psend.at[p], precv.at[p], other)
+        score[p] = part[0:64]
+        dl[p, :, 0:FFD] = gate_delta[0:64].astype(BF16)
+        dl[p, :, FFD:2 * FFD] = up_delta[0:64].astype(BF16)
         dlt[0:FFD, at:at + ROWS] = gate_delta.T.astype(BF16)
         dlt[FFD:2 * FFD, at:at + ROWS] = up_delta.T.astype(BF16)
         hidt[:, at:at + ROWS] = hidden.T.astype(BF16)
@@ -296,14 +296,14 @@
         def _(t):
             cols = pl.ds(pl.multiple_of(t * 512, 512), 512)
             grad = contract_cols(mine, wgu[cols, :]) + contract_cols(theirs, wgup[cols, :])
-            rgf[p % 2, :, cols] = grad[0:48]
+            rgf[p % 3, :, cols] = grad[0:48]
             o3s[p, :, cols] = grad[48:64].astype(BF16)
             ready[p, :, cols] = grad[16:32].astype(BF16) if ready is j1s else grad[32:48].astype(BF16)
 
     def row_left(p):
         back[p, "c"].wait_recv()
         total = score[p] + from_hi_lo(precv[p, :, 2 * FFD:])
-        rgf[p % 2, :, D:] = total[0:48]
+        rgf[p % 3, :, D:] = total[0:48]
         o3s[p, :, D:] = hi_lo(total[48:64])
         j2s[p, :, D:] = hi_lo(total[32:48])
         row_tiles(p, 0, 7, j1s)
@@ -327,11 +327,11 @@
 
     def merge(p):
         back[p, "ol"].wait_recv()
-        j2s[p, :, 0:HALF] = (rgf[p % 2, 32:48, 0:HALF] + o3r[p, :, 0:HALF].astype(F32)).astype(BF16)
+        j2s[p, :, 0:HALF] = (rgf[p % 3, 32:48, 0:HALF] + o3r[p, :, 0:HALF].astype(F32)).astype(BF16)
         back[p, "j2l"] = send(j2s.at[p, :, left], j2r.at[p, :, left], up)
         back[p, "or"].wait_recv()
-        j1s[p, :, HALF:D] = (rgf[p % 2, 16:32, HALF:D] + o3r[p, :, HALF:D].astype(F32)).astype(BF16)
-        j1s[p, :, D:] = hi_lo(rgf[p % 2, 16:32, D:] + from_hi_lo(o3r[p, :, D:]))
+        j1s[p, :, HALF:D] = (rgf[p % 3, 16:32, HALF:D] + o3r[p, :, HALF:D].astype(F32)).astype(BF16)
+        j1s[p, :, D:] = hi_lo(rgf[p % 3, 16:32, D:] + from_hi_lo(o3r[p, :, D:]))
         back[p, "j1r"] = send(j1s.at[p, :, tail], j1r.at[p, :, tail], down)
 
     def home(p):
@@ -339,9 +339,9 @@
             back[p, part].wait_recv()
         for q in range(4):
             cols = slice(q * QUART, (q + 1) * QUART)
-            full = rgf[p % 2, 0:16, cols] + j1r[p, :, cols].astype(F32) + j2r[p, :, cols].astype(F32)
+            full = rgf[p % 3, 0:16, cols] + j1r[p, :, cols].astype(F32) + j2r[p, :, cols].astype(F32)
             fstk[16 * q:16 * q + 16, 0:QUART] = full.astype(BF16)
-        total = hi_lo(rgf[p % 2, 0:16, D:] + from_hi_lo(j1r[p, :, D:]) + from_hi_lo(j2r[p, :, D:]))
+        total = hi_lo(rgf[p % 3, 0:16, D:] + from_hi_lo(j1r[p, :, D:]) + from_hi_lo(j2r[p, :, D:]))
         for q in range(4):
             fstk[16 * q:16 * q + 16, QUART:] = total
         block = jnp.dot(perm[...], fstk[...], preferred_element_type=F32).astype(BF16)
@@ -352,6 +352,49 @@
             if k:
                 part = pl.ds(16 * k, 16)
                 back[k] = send(rets.at[part], retr.at[part], source(k))
+
+    def half_quarter(q, piece, score):
+        at = q * QUART + piece * (QUART // 2)
+        return slice(at, at + QUART // 2 + (SCW if score else 0))
+
+    def merge_pieces(p):
+        for piece in range(2):
+            if piece == 0:
+                back[p, "ol"].wait_recv()
+            for q in range(2):
+                cols = half_quarter(q, piece, False)
+                j2s[p, :, cols] = (rgf[p % 3, 32:48, cols] + o3r[p, :, cols].astype(F32)).astype(BF16)
+                back[p, "j2l", piece, q] = send(j2s.at[p, :, cols], j2r.at[p, :, cols], up)
+            if piece == 0:
+                back[p, "or"].wait_recv()
+            for q in range(2, 4):
+                cols = half_quarter(q, piece, False)
+                j1s[p, :, cols] = (rgf[p % 3, 16:32, cols] + o3r[p, :, cols].astype(F32)).astype(BF16)
+                score_too = piece == 1 and q == 3
+                if score_too:
+                    j1s[p, :, D:] = hi_lo(rgf[p % 3, 16:32, D:] + from_hi_lo(o3r[p, :, D:]))
+                cols = half_quarter(q, piece, score_too)
+                back[p, "j1r", piece, q] = send(j1s.at[p, :, cols], j1r.at[p, :, cols], down)
+
+    def home_piece(p, piece):
+        if piece == 0:
+            back[p, "j1l"].wait_recv()
+            back[p, "j2r"].wait_recv()
+        for q in range(4):
+            back[(p, "j2l", piece, q) if q < 2 else (p, "j1r", piece, q)].wait_recv()
+            cols = half_quarter(q, piece, False)
+            full = rgf[p % 3, 0:16, cols] + j1r[p, :, cols].astype(F32) + j2r[p, :, cols].astype(F32)
+            fstk[16 * q:16 * q + 16, half_quarter(0, piece, False)] = full.astype(BF16)
+        if piece == 1:
+            total = hi_lo(rgf[p % 3, 0:16, D:] + from_hi_lo(j1r[p, :, D:]) + from_hi_lo(j2r[p, :, D:]))
+            for q in range(4):
+                fstk[16 * q:16 * q + 16, QUART:] = total
+        cols = half_quarter(0, piece, piece == 1)
+        block = jnp.dot(perm[...], fstk[:, cols], preferred_element_type=F32).astype(BF16)
+        rets[64 * p:64 * p + 64, cols] = block
+        for k in range(4 * p, 4 * p + 4):
+            part = pl.ds(16 * k, 16)
+            back[k, piece] = send(rets.at[part, cols], retr.at[part, cols], source(k))
 
     def weight_grads(lo, hi):
         @pl.loop(lo, hi)
@@ -415,18 +458,23 @@
     send_left(2)
     send_right(2)
     compute(3)
-    home(1)
+    merge(2)
     row_left(3)
     send_left(3)
     row_right(3)
     send_right(3)
-    merge(2)
+    home(1)
     home(2)
-    merge(3)
-    weight_grads(0, 14)
-    home(3)
-    for k in range(1, NODES):
+    merge_pieces(3)
+    weight_grads(0, 6)
+    home_piece(3, 0)
+    home_piece(3, 1)
+    weight_grads(6, 14)
+    for k in range(1, 12):
         back[k].wait_recv()
+    for k in range(12, NODES):
+        back[k, 0].wait_recv()
+        back[k, 1].wait_recv()
     for copy in remote:
         copy.wait_send()
 
@@ -465,7 +513,7 @@
     any_space = pl.BlockSpec(memory_space=pl.ANY)
     in_vmem = pl.BlockSpec(memory_space=pltpu.VMEM)
     ids, gates = route_ids.T, route_gates.T
-    copies = 30 + 8 * 7 + 6 + 4 + 4 * 6 + 15 + 1
+    copies = 30 + 8 * 7 + 6 + 4 + 4 * 6 + 15 + 1 + 10
     ret, gg, gu, gd = pl.pallas_call(
         exchange_kernel,
         out_shape=(
@@ -495,7 +543,7 @@
             pltpu.VMEM((PH, 64, SCW), F32),
             pltpu.VMEM((PH, 64, 2 * FFD + SCW), BF16),
             pltpu.VMEM((PH, 64, 2 * FFD + SCW), BF16),
-            pltpu.VMEM((2, 48, RW), F32),
+            pltpu.VMEM((3, 48, RW), F32),
             pltpu.VMEM((PH, 16, RW), BF16),
             pltpu.VMEM((PH, 16, RW), BF16),
             pltpu.VMEM((PH, 16, RW), BF16),
@@ -511,7 +559,7 @@
             pltpu.SemaphoreType.DMA((9,)),
         ],
         compiler_params=pltpu.CompilerParams(
-            collective_id=0, has_side_effects=True, vmem_limit_bytes=50 * 2**20
+            collective_id=0, has_side_effects=True, vmem_limit_bytes=52 * 2**20
         ),
         cost_estimate=pl.CostEstimate(
             flops=8 * 10**9, bytes_accessed=20 * 10**6, transcendentals=65536

time: 127 us -> 125 us (0.984)
  Pallas kernels: 122 us -> 120 us
    pallas_call x1, Pallas kernels: 119 us -> 117 us  [body(): pl.pallas_call(exchange_kernel, out_shape=(pltpu.VMEM((TOK, QUART + SCW),...]
where the time goes in v3:
time: 125 us; the launch traced here: 124 us
  Pallas kernels  120 us (96%)
  local copies, waits for them, and re-layouts  3.69 us (3%)
    pallas_call x1, Pallas kernels, body(): pl.pallas_call(exchange_kernel, out_shape=(pltpu.VMEM((TOK, QUART + SCW),...  117 us
    unnamed x7, local copies, waits for them, and re-layouts  3.69 us
    pallas_call x1, Pallas kernels, body(): pl.pallas_call(scatter_kernel, out_shape=(jax.ShapeDtypeStruct((TOK, D),...  3.09 us

profile of v3, /device:TPU:0, one launch (start us, length us, event | category | flops | bytes accessed | tf_op | source)
XLA Modules:
  0.0 124.0 jit_solution(2455829352073260421)
XLA Ops:
  0.6 116.6 %exchange.1 = (bf16[256,1920]{1,0:T(8,128)(2,1)S(1)}, bf16[7168,128]{1,0:T(8,128)(2,1)S(1)}, bf16[7168,128]{1,0:T(8,128)(2,1)S(1)}, bf16[128,7168]{1,0:T(8,128)(2,1)S(1)}) custom-call(s32[8,256]{1,0:T(8,128)} %bitcast.12, bf16[8,256]{1,0:T(8,128)(2,1)} %bitcast.14, bf16[256,7168]{1,0:T(8,128)(2,1)} %tok_hbm.1, bf16[256,7168]{1,0:T(8,128)(2,1)} %og_hbm.1, ...), custom_call_target="tpu_custom_call" | custom-call | flops 8000000000 | bytes 20000000 | tf_op jit(solution)/shard_map/exchange/pallas_call | solution.py:517
  117.2 1.2 copy.15
  118.5 1.2 copy.16
  119.7 0.0 copy-start
  119.7 0.0 copy-start.1
  119.7 1.2 copy.17
  120.9 0.0 copy-done
  120.9 0.0 copy-done.1
  120.9 3.1 %scatter.1 = (bf16[256,7168]{1,0:T(8,128)(2,1)}, f32[8,256]{1,0:T(8,128)}) custom-call(s32[8,256]{1,0:T(8,128)S(1)} %bitcast.13, bf16[8,256]{1,0:T(8,128)(2,1)S(1)} %bitcast.15, bf16[256,1920]{1,0:T(8,128)(2,1)S(1)} %get-tuple-element.11.ret), custom_call_target="tpu_custom_call" | custom-call | tf_op jit(solution)/shard_map/scatter/pallas_call | solution.py:569
Async XLA Ops:
  119.7 1.2 copy-start
  119.7 1.2 copy-start.1

commit v4 on v3

--- a/solution.py
+++ b/solution.py
@@ -81,7 +81,7 @@
 
 def exchange_kernel(
     ids_hbm, gates_hbm, tok_hbm, og_hbm, wg_hbm, wu_hbm, wd_hbm,
-    retr, ggo, guo, gdo,
+    retr, gguo, gdo,
     ids, gates, tok, og, pick, sraw, rraw, rx, xg, wgu, wgup, wd,
     dl, dlt, hidt, score, psend, precv,
     rgf, o3s, o3r, j1s, j1r, j2s, j2r, fstk, rets, perm, pre_ref,
@@ -401,8 +401,8 @@
         def _(t):
             cols = pl.ds(pl.multiple_of(t * 512, 512), 512)
             both = jnp.dot(dlt[...], xg[0, :, cols], preferred_element_type=F32)
-            ggo[cols, :] = both[0:FFD].T.astype(BF16)
-            guo[cols, :] = both[FFD:].T.astype(BF16)
+            gguo[cols, :] = both[0:FFD].T.astype(BF16)
+            gguo[pl.ds(pl.multiple_of(D + t * 512, 512), 512), :] = both[FFD:].T.astype(BF16)
             gdo[:, cols] = jnp.dot(hidt[...], xg[1, :, cols], preferred_element_type=F32).astype(BF16)
 
     send_part(2)
@@ -479,7 +479,7 @@
         copy.wait_send()
 
 
-def scatter_kernel(ids, gates, ret, grad_hbm, gate_grad, grad, sem):
+def scatter_kernel(ids, gates, ret, ggu, gd_in, grad_hbm, gate_grad, gg, gu, gd, grad, sem):
     copies = []
 
     def start(src, dst):
@@ -487,6 +487,9 @@
         copies.append(copy)
         copy.start()
 
+    start(ggu.at[pl.ds(0, D)], gg)
+    start(ggu.at[pl.ds(D, D)], gu)
+    start(gd_in, gd)
     node = lax.axis_index("node")
     gx, gz = node // SIDE, node % SIDE
     target, gate = slot_targets(ids[...], gates[...])
@@ -514,16 +517,15 @@
     in_vmem = pl.BlockSpec(memory_space=pltpu.VMEM)
     ids, gates = route_ids.T, route_gates.T
     copies = 30 + 8 * 7 + 6 + 4 + 4 * 6 + 15 + 1 + 10
-    ret, gg, gu, gd = pl.pallas_call(
+    ret, ggu, gd = pl.pallas_call(
         exchange_kernel,
         out_shape=(
             pltpu.VMEM((TOK, QUART + SCW), BF16),
-            pltpu.VMEM((D, FFD), BF16),
-            pltpu.VMEM((D, FFD), BF16),
+            pltpu.VMEM((2 * D, FFD), BF16),
             pltpu.VMEM((FFD, D), BF16),
         ),
         in_specs=[any_space] * 7,
-        out_specs=(in_vmem,) * 4,
+        out_specs=(in_vmem,) * 3,
         scratch_shapes=[
             pltpu.VMEM((8, TOK), jnp.int32),
             pltpu.VMEM((8, TOK), BF16),
@@ -566,21 +568,24 @@
         ),
         name="exchange",
     )(ids, gates, tokens, out_grad, w_gate[0], w_up[0], w_down[0])
-    token_grad, gate_grad = pl.pallas_call(
+    token_grad, gate_grad, gg, gu, gd = pl.pallas_call(
         scatter_kernel,
         out_shape=(
             jax.ShapeDtypeStruct((TOK, D), BF16),
             jax.ShapeDtypeStruct((8, TOK), F32),
+            jax.ShapeDtypeStruct((D, FFD), BF16),
+            jax.ShapeDtypeStruct((D, FFD), BF16),
+            jax.ShapeDtypeStruct((FFD, D), BF16),
         ),
-        in_specs=[in_vmem] * 3,
-        out_specs=(any_space, in_vmem),
+        in_specs=[in_vmem] * 5,
+        out_specs=(any_space, in_vmem) + (any_space,) * 3,
         scratch_shapes=[
             pltpu.VMEM((TOK, D), BF16),
-            pltpu.SemaphoreType.DMA((4,)),
+            pltpu.SemaphoreType.DMA((7,)),
         ],
         compiler_params=pltpu.CompilerParams(vmem_limit_bytes=16 * 2**20),
         name="scatter",
-    )(ids, gates, pltpu.with_memory_space_constraint(ret, pltpu.VMEM))
+    )(ids, gates, *(pltpu.with_memory_space_constraint(x, pltpu.VMEM) for x in (ret, ggu, gd)))
     return token_grad, gate_grad.T, gg[None], gu[None], gd[None]
 
 

time: 125 us -> 122 us (0.976)
  local copies, waits for them, and re-layouts: 3.69 us -> 0.01 us
    unnamed x7 -> x4, local copies, waits for them, and re-layouts: 3.69 us -> 0.01 us
    pallas_call x1, Pallas kernels: 3.09 us -> 4.41 us  [body(): pl.pallas_call(scatter_kernel, out_shape=(jax.ShapeDtypeStruct((TOK, D),...]
where the time goes in v4:
time: 122 us
  Pallas kernels  121 us (99%)
    pallas_call x1, Pallas kernels, body(): pl.pallas_call(exchange_kernel, out_shape=(pltpu.VMEM((TOK, QUART + SCW),...  117 us
    pallas_call x1, Pallas kernels, body(): pl.pallas_call(scatter_kernel, out_shape=(jax.ShapeDtypeStruct((TOK, D),...  4.41 us

profile of v4, /device:TPU:0, one launch (start us, length us, event | category | flops | bytes accessed | tf_op | source)
XLA Modules:
  0.0 121.7 jit_solution(11875648978037761651)
XLA Ops:
  0.6 0.0 copy-start
  0.6 0.0 copy-start.1
  0.7 116.6 %exchange.1 = (bf16[256,1920]{1,0:T(8,128)(2,1)S(1)}, bf16[14336,128]{1,0:T(8,128)(2,1)S(1)}, bf16[128,7168]{1,0:T(8,128)(2,1)S(1)}) custom-call(s32[8,256]{1,0:T(8,128)} %bitcast.9, bf16[8,256]{1,0:T(8,128)(2,1)} %bitcast.11, bf16[256,7168]{1,0:T(8,128)(2,1)} %tok_hbm.1, bf16[256,7168]{1,0:T(8,128)(2,1)} %og_hbm.1, bf16[7168,128]{1,0:T(8,128)(2,1)} %bitcast.13, ...), custom_call_target="tpu_custom_call" | custom-call | flops 8000000000 | bytes 20000000 | tf_op jit(solution)/shard_map/exchange/pallas_call | solution.py:520
  117.2 0.0 copy-done
  117.3 0.0 copy-done.1
  117.3 4.4 %scatter.1 = (bf16[256,7168]{1,0:T(8,128)(2,1)}, f32[8,256]{1,0:T(8,128)}, bf16[7168,128]{1,0:T(8,128)(2,1)}, bf16[7168,128]{1,0:T(8,128)(2,1)}, bf16[128,7168]{1,0:T(8,128)(2,1)}) custom-call(s32[8,256]{1,0:T(8,128)S(1)} %bitcast.10, bf16[8,256]{1,0:T(8,128)(2,1)S(1)} %bitcast.12, bf16[256,1920]{1,0:T(8,128)(2,1)S(1)} %get-tuple-element.13.ret, ...), custom_call_target="tpu_custom_call" | custom-call | tf_op jit(solution)/shard_map/scatter/pallas_call | solution.py:571
Async XLA Ops:
  0.6 116.6 %copy-start = (s32[256,8]{0,1:T(8,128)S(1)}, s32[256,8]{0,1:T(8,128)}, u32[]{:S(2)}) copy-start(s32[256,8]{0,1:T(8,128)} %param.9) | copy-start | bytes 24580
  0.6 116.6 %copy-start.1 = (bf16[256,8]{0,1:T(8,128)(2,1)S(1)}, bf16[256,8]{0,1:T(8,128)(2,1)}, u32[]{:S(2)}) copy-start(bf16[256,8]{0,1:T(8,128)(2,1)} %param.10) | copy-start | bytes 12292

commit v5 on v4

--- a/solution.py
+++ b/solution.py
@@ -466,10 +466,10 @@
     home(1)
     home(2)
     merge_pieces(3)
-    weight_grads(0, 6)
+    weight_grads(0, 10)
     home_piece(3, 0)
     home_piece(3, 1)
-    weight_grads(6, 14)
+    weight_grads(10, 14)
     for k in range(1, 12):
         back[k].wait_recv()
     for k in range(12, NODES):

time: 122 us -> 122 us (level)
  no operation moved by 1% of the time
where the time goes in v5:
time: 122 us
  Pallas kernels  121 us (99%)
    pallas_call x1, Pallas kernels, body(): pl.pallas_call(exchange_kernel, out_shape=(pltpu.VMEM((TOK, QUART + SCW),...  117 us
    pallas_call x1, Pallas kernels, body(): pl.pallas_call(scatter_kernel, out_shape=(jax.ShapeDtypeStruct((TOK, D),...  4.41 us

profile of v5, /device:TPU:0, one launch (start us, length us, event | category | flops | bytes accessed | tf_op | source)
XLA Modules:
  0.0 121.7 jit_solution(15189002289970233695)
XLA Ops:
  0.6 0.0 copy-start
  0.6 0.0 copy-start.1
  0.7 116.6 %exchange.1 = (bf16[256,1920]{1,0:T(8,128)(2,1)S(1)}, bf16[14336,128]{1,0:T(8,128)(2,1)S(1)}, bf16[128,7168]{1,0:T(8,128)(2,1)S(1)}) custom-call(s32[8,256]{1,0:T(8,128)} %bitcast.9, bf16[8,256]{1,0:T(8,128)(2,1)} %bitcast.11, bf16[256,7168]{1,0:T(8,128)(2,1)} %tok_hbm.1, bf16[256,7168]{1,0:T(8,128)(2,1)} %og_hbm.1, bf16[7168,128]{1,0:T(8,128)(2,1)} %bitcast.13, ...), custom_call_target="tpu_custom_call" | custom-call | flops 8000000000 | bytes 20000000 | tf_op jit(solution)/shard_map/exchange/pallas_call | solution.py:520
  117.2 0.0 copy-done
  117.3 0.0 copy-done.1
  117.3 4.4 %scatter.1 = (bf16[256,7168]{1,0:T(8,128)(2,1)}, f32[8,256]{1,0:T(8,128)}, bf16[7168,128]{1,0:T(8,128)(2,1)}, bf16[7168,128]{1,0:T(8,128)(2,1)}, bf16[128,7168]{1,0:T(8,128)(2,1)}) custom-call(s32[8,256]{1,0:T(8,128)S(1)} %bitcast.10, bf16[8,256]{1,0:T(8,128)(2,1)S(1)} %bitcast.12, bf16[256,1920]{1,0:T(8,128)(2,1)S(1)} %get-tuple-element.13.ret, ...), custom_call_target="tpu_custom_call" | custom-call | tf_op jit(solution)/shard_map/scatter/pallas_call | solution.py:571
Async XLA Ops:
  0.6 116.6 %copy-start = (s32[256,8]{0,1:T(8,128)S(1)}, s32[256,8]{0,1:T(8,128)}, u32[]{:S(2)}) copy-start(s32[256,8]{0,1:T(8,128)} %param.9) | copy-start | bytes 24580
  0.6 116.6 %copy-start.1 = (bf16[256,8]{0,1:T(8,128)(2,1)S(1)}, bf16[256,8]{0,1:T(8,128)(2,1)}, u32[]{:S(2)}) copy-start(bf16[256,8]{0,1:T(8,128)(2,1)} %param.10) | copy-start | bytes 12292
